TPU v7x, 512 devices: a whole 4x4x16 slice. The times are simulated.
512 devices in a mesh: row: 32 (over z, core), col: 16 (over x, y).
Axes of the slice: x: 4, y: 4, z: 16, core: 2. Of those that a mesh axis runs over, the one named last changes fastest.
Arguments:
- inputs: bfloat16 [384, 14848], P('row', 'col'), may hold values from -6 to 6
- out_grad: bfloat16 [384, 14848], P('col', 'row'), may hold values from -6 to 6
- w_up: bfloat16 [14848, 14848], P('col', 'row'), may hold values from -0.046875 to 0.046875
- w_down: bfloat16 [14848, 14848], P('col', 'row'), may hold values from -0.046875 to 0.046875
Outputs:
- input_grad: bfloat16 [384, 14848], P('row', 'col')
- up_grad: float32 [14848, 14848], P('col', 'row')
- down_grad: float32 [14848, 14848], P('col', 'row')
All inputs are finite; a program needn't handle non-finite values.
Results may differ from a plain program's by a relative error of at most 0.0049.
Values may be sent and summed in bfloat16 or wider, within the bound.
A program may use at most 64 MiB of HBM per device.

v0:
```python
import math

import jax
import jax.numpy as jnp
from jax import lax
from jax.sharding import PartitionSpec as P


def spread(value, axis, root):
    mine = lax.axis_index(axis) == root
    return lax.psum(jnp.where(mine, value, jnp.zeros_like(value)), axis)


def gelu_parts(hidden):
    cdf = 0.5 * (1.0 + jax.scipy.special.erf(hidden / math.sqrt(2.0)))
    pdf = jnp.exp(-0.5 * hidden * hidden) / math.sqrt(2.0 * math.pi)
    return (cdf, pdf)


def shards(inputs, out_grad, w_up, w_down):
    row_index = lax.axis_index("row")
    col_index = lax.axis_index("col")
    gathered = lax.all_gather(inputs, "row", axis=0, tiled=True)
    hidden_part = jnp.dot(gathered, w_up, preferred_element_type=jnp.float32)
    hidden_rows = lax.psum(hidden_part, "col")
    width = hidden_rows.shape[1]
    pieces = []
    for half in range(2):
        pieces.append(spread(hidden_rows, "row", 2 * col_index + half))
    hidden_cols = jnp.concatenate(pieces, 1)
    cdf, pdf = gelu_parts(hidden_cols)
    activation = (hidden_cols * cdf).astype(jnp.bfloat16)
    slope = cdf + hidden_cols * pdf
    dy_rows = lax.all_gather(out_grad, "col", axis=0, tiled=True)
    down_grad = lax.dot_general(
        activation, dy_rows, (((0,), (0,)), ((), ())), preferred_element_type=jnp.float32
    )
    act_part = lax.dot_general(
        dy_rows, w_down, (((1,), (1,)), ((), ())), preferred_element_type=jnp.float32
    )
    act_grad = lax.psum(act_part, "row")
    hidden_grad = (act_grad * slope).astype(jnp.bfloat16)
    own_half = lax.dynamic_slice_in_dim(hidden_grad, row_index % 2 * width, width, 1)
    grad_rows = spread(own_half, "col", row_index // 2)
    up_grad = lax.dot_general(
        gathered, grad_rows, (((0,), (0,)), ((), ())), preferred_element_type=jnp.float32
    )
    input_grad = lax.psum_scatter(
        lax.dot_general(
            grad_rows, w_up, (((1,), (1,)), ((), ())), preferred_element_type=jnp.float32
        ),
        "row",
        scatter_dimension=0,
        tiled=True,
    )
    return (input_grad.astype(jnp.bfloat16), up_grad, down_grad)


def solution(mesh):
    return jax.shard_map(
        shards,
        mesh=mesh,
        in_specs=(P("row", "col"), P("col", "row"), P("col", "row"), P("col", "row")),
        out_specs=(P("row", "col"), P("col", "row"), P("col", "row")),
        check_vma=False,
    )
```

profile of v0, /device:TPU:1, one launch (start us, length us, event | category | flops | bytes accessed | tf_op | source)
XLA Modules:
  0.0 606.9 jit_solution(17880862676471831035)
XLA Ops:
  7.2 40.8 %all-gather = bf16[32,12,928]{2,1,0:T(8,128)(2,1)S(1)} all-gather(bf16[1,12,928]{2,1,0:T(8,128)(2,1)} %bitcast.15), channel_id=1, replica_groups=mesh['row'=32,'col'=16] {'row'}, dimensions={0}, use_global_device_ids=true | all-gather | bytes 734976 | tf_op jit(solution)/shard_map/all_gather | solution.py:23
  48.0 0.4 reshape.7
  48.5 1.6 fusion.7
  50.1 0.0 all-reduce.11.cloned.1.call-start
  50.2 20.0 %all_gather.6 = bf16[384,464]{1,0:T(8,128)(2,1)S(1)} all-gather(bf16[24,464]{1,0:T(8,128)(2,1)S(1)} %copy-done.8), channel_id=1, replica_groups=mesh['row'=32,'col'=16] {'col'}, dimensions={0}, use_global_device_ids=true | all-gather | bytes 378624 | tf_op jit(solution)/shard_map/all_gather | solution.py:34
  70.2 1.8 fusion.6
  71.9 88.5 %all-reduce.7.cloned.1.call-done = f32[384,464]{0,1:T(8,128)} async-done(((f32[384,464]{0,1:T(8,128)}), f32[384,464]{0,1:T(8,128)}) %all-reduce.7.cloned.1.call-update) | async-done | bytes 712720 | tf_op jit(solution)/shard_map/psum | solution.py:25
  160.4 2.3 broadcast_select_fusion
  162.8 218.7 %all-reduce.11.cloned.1.call-done = (f32[384,464]{0,1:T(8,128)}, f32[384,464]{0,1:T(8,128)}, f32[384,928]{0,1:T(8,128)}) async-done(((f32[384,464]{0,1:T(8,128)}, f32[384,464]{0,1:T(8,128)}, f32[384,928]{0,1:T(8,128)}), (f32[384,464]{0,1:T(8,128)}, f32[384,464]{0,1:T(8,128)}, f32[384,928]{0,1:T(8,128)})) %all-reduce.11.cloned.1.call-update) | async-done | bytes 2850832 | tf_op jit(solution)/shard_map/psum | solution.py:11
  381.6 1.2 constant_dynamic-update-slice_fusion.1
  382.8 0.1 copy-done.6
  382.9 0.3 add_multiply_fusion
  383.2 1.1 copy-done.1
  384.3 0.2 copy-done.7
  384.5 1.0 fusion.4
  385.5 1.3 dynamic-slice.4
  387.5 111.9 %all-reduce.9.cloned.1.call-done = bf16[384,464]{0,1:T(8,128)(2,1)} async-done(((bf16[384,464]{0,1:T(8,128)(2,1)}), bf16[384,464]{0,1:T(8,128)(2,1)}) %all-reduce.9.cloned.1.call-update) | async-done | bytes 356368 | tf_op jit(solution)/shard_map/psum | solution.py:11
  499.3 2.7 fusion.8
  502.1 59.9 %fusion = f32[16,928]{1,0:T(8,128)S(1)} fusion(f32[384,928]{1,0:T(8,128)} %fusion.8), kind=kCustom, calls=%all-reduce-scatter | all-reduce-scatter fusion | flops 475137 | bytes 1486848
  562.0 6.9 %collective-permute-start.6 = (bf16[16,928]{1,0:T(8,128)(2,1)S(1)}, bf16[16,928]{1,0:T(8,128)(2,1)S(1)}, u32[]{:S(2)}, u32[]{:S(2)}) collective-permute-start(bf16[16,928]{1,0:T(8,128)(2,1)S(1)} %convert.14), channel_id=1, source_target_pairs={{0,112},{16,128},{32,144},{48,160},{64,176},{80,192},{96,208},{112... | collective-permute-start | bytes 89096
  568.9 3.5 collective-permute-start.5
  572.4 6.4 %collective-permute-start.7 = (bf16[12,928]{1,0:T(8,128)(2,1)S(1)}, bf16[12,928]{1,0:T(8,128)(2,1)S(1)}, u32[]{:S(2)}, u32[]{:S(2)}) collective-permute-start(bf16[12,928]{1,0:T(8,128)(2,1)S(1)} %slice), channel_id=1, source_target_pairs={{0,128},{16,144},{32,160},{48,176},{64,192},{80,208},{96,224},{112... | collective-permute-start | bytes 66824
  578.8 3.3 fusion.1
  582.1 1.3 collective-permute-start.4
  583.4 6.1 %collective-permute-start.3 = (bf16[16,928]{1,0:T(8,128)(2,1)S(1)}, bf16[16,928]{1,0:T(8,128)(2,1)S(1)}, u32[]{:S(2)}, u32[]{:S(2)}) collective-permute-start(bf16[16,928]{1,0:T(8,128)(2,1)S(1)} %convert.14), channel_id=1, source_target_pairs={{0,64},{16,80},{32,96},{48,112},{64,128},{80,144},{96,160},{112,17... | collective-permute-start | bytes 89096
  589.5 1.6 collective-permute-start.2
  591.2 2.8 collective-permute-start.1
  594.0 2.2 collective-permute-start
  596.2 0.7 convolution_bitcast_fusion
  596.8 1.7 copy.9
  598.6 1.2 concatenate.4
  599.8 0.6 dynamic-slice_convert_fusion
  (31 shorter events, 0.3 us)
Async XLA Ops:
  7.2 41.3 %copy-start = (bf16[928,464]{1,0:T(8,128)(2,1)S(1)}, bf16[928,464]{1,0:T(8,128)(2,1)}, u32[]{:S(2)}) copy-start(bf16[928,464]{1,0:T(8,128)(2,1)} %param.6) | copy-start | bytes 2583556
  7.2 153.3 %all-reduce.7.cloned.1.call-start = ((), (), s32[]{:S(2)}) async-start(), calls=%async_computation | async-start | bytes 1425408 | tf_op jit(solution)/shard_map/psum | solution.py:25
  48.4 1.6 copy-start.2
  48.5 1.7 copy-start.8
  48.5 21.7 %copy-start.5 = (bf16[928,464]{1,0:T(8,128)(2,1)S(1)}, bf16[928,464]{1,0:T(8,128)(2,1)}, u32[]{:S(2)}) copy-start(bf16[928,464]{1,0:T(8,128)(2,1)} %param.7) | copy-start | bytes 2583556
  50.1 331.5 %all-reduce.11.cloned.1.call-start = ((), (), s32[]{:S(2)}) async-start(), calls=%async_computation.2 | async-start | bytes 5701632 | tf_op jit(solution)/shard_map/psum | solution.py:11
  162.8 336.6 %all-reduce.9.cloned.1.call-start = ((), (), s32[]{:S(2)}) async-start(), calls=%async_computation.1 | async-start | bytes 712704 | tf_op jit(solution)/shard_map/psum | solution.py:11
  381.6 1.3 copy-start.6
  382.9 1.6 copy-start.7
  383.2 1.1 copy-start.1
  562.0 34.2 %copy-start.3 = (bf16[384,928]{1,0:T(8,128)(2,1)S(1)}, bf16[384,928]{1,0:T(8,128)(2,1)}, u32[]{:S(2)}) copy-start(bf16[384,928]{1,0:T(8,128)(2,1)} %copy-done.2) | copy-start | bytes 2138116
  562.0 34.2 %copy-start.4 = (bf16[384,464]{0,1:T(8,128)(2,1)S(1)}, bf16[384,464]{0,1:T(8,128)(2,1)}, u32[]{:S(2)}) copy-start(bf16[384,464]{0,1:T(8,128)(2,1)} %all-reduce.9.cloned.1.call-done) | copy-start | bytes 1069060
  562.0 29.2 %collective-permute-start.6 = (bf16[16,928]{1,0:T(8,128)(2,1)S(1)}, bf16[16,928]{1,0:T(8,128)(2,1)S(1)}, u32[]{:S(2)}, u32[]{:S(2)}) collective-permute-start(bf16[16,928]{1,0:T(8,128)(2,1)S(1)} %convert.14), channel_id=1, source_target_pairs={{0,112},{16,128},{32,144},{48,160},{64,176},{80,192},{96,208},{112... | collective-permute-start | bytes 89096
  568.9 25.1 %collective-permute-start.5 = (bf16[16,928]{1,0:T(8,128)(2,1)S(1)}, bf16[16,928]{1,0:T(8,128)(2,1)S(1)}, u32[]{:S(2)}, u32[]{:S(2)}) collective-permute-start(bf16[16,928]{1,0:T(8,128)(2,1)S(1)} %convert.14), channel_id=1, source_target_pairs={{0,96},{16,112},{32,128},{48,144},{64,160},{80,176},{96,192},{112,... | collective-permute-start | bytes 89096
  572.4 17.1 %collective-permute-start.7 = (bf16[12,928]{1,0:T(8,128)(2,1)S(1)}, bf16[12,928]{1,0:T(8,128)(2,1)S(1)}, u32[]{:S(2)}, u32[]{:S(2)}) collective-permute-start(bf16[12,928]{1,0:T(8,128)(2,1)S(1)} %slice), channel_id=1, source_target_pairs={{0,128},{16,144},{32,160},{48,176},{64,192},{80,208},{96,224},{112... | collective-permute-start | bytes 66824
  582.1 16.5 %collective-permute-start.4 = (bf16[16,928]{1,0:T(8,128)(2,1)S(1)}, bf16[16,928]{1,0:T(8,128)(2,1)S(1)}, u32[]{:S(2)}, u32[]{:S(2)}) collective-permute-start(bf16[16,928]{1,0:T(8,128)(2,1)S(1)} %convert.14), channel_id=1, source_target_pairs={{0,80},{16,96},{32,112},{48,128},{64,144},{80,160},{96,176},{112,1... | collective-permute-start | bytes 89096
  583.4 15.2 %collective-permute-start.3 = (bf16[16,928]{1,0:T(8,128)(2,1)S(1)}, bf16[16,928]{1,0:T(8,128)(2,1)S(1)}, u32[]{:S(2)}, u32[]{:S(2)}) collective-permute-start(bf16[16,928]{1,0:T(8,128)(2,1)S(1)} %convert.14), channel_id=1, source_target_pairs={{0,64},{16,80},{32,96},{48,112},{64,128},{80,144},{96,160},{112,17... | collective-permute-start | bytes 89096
  589.5 9.1 %collective-permute-start.2 = (bf16[16,928]{1,0:T(8,128)(2,1)S(1)}, bf16[16,928]{1,0:T(8,128)(2,1)S(1)}, u32[]{:S(2)}, u32[]{:S(2)}) collective-permute-start(bf16[16,928]{1,0:T(8,128)(2,1)S(1)} %convert.14), channel_id=1, source_target_pairs={{0,48},{16,64},{32,80},{48,96},{64,112},{80,128},{96,144},{112,160... | collective-permute-start | bytes 89096
  591.2 7.4 %collective-permute-start.1 = (bf16[16,928]{1,0:T(8,128)(2,1)S(1)}, bf16[16,928]{1,0:T(8,128)(2,1)S(1)}, u32[]{:S(2)}, u32[]{:S(2)}) collective-permute-start(bf16[16,928]{1,0:T(8,128)(2,1)S(1)} %convert.14), channel_id=1, source_target_pairs={{0,32},{16,48},{32,64},{48,80},{64,96},{80,112},{96,128},{112,144}... | collective-permute-start | bytes 89096
  594.0 4.6 collective-permute-start
Sparse Core Ops, SparseCore 0:
  50.2 110.1 all-reduce.6
  163.6 217.9 all-reduce.10
  385.7 113.6 all-reduce.8
where the time goes:
time: 608 us; the launch traced here: 607 us
  waiting for transfers between devices  419 us (69%)
  blocking collectives  121 us (20%)
  starting transfers between devices  30.9 us (5%)
  between operations  14.7 us (2%)
  matrix products  10 us (2%)
  local copies, waits for them, and re-layouts  7.92 us (1%)
    psum x2, waiting for transfers between devices, spread(): return lax.psum(jnp.where(mine, value, jnp.zeros_like(value)), axis)  331 us
    psum x1, waiting for transfers between devices, shards(): hidden_rows = lax.psum(hidden_part, 'col')  88.5 us
    unnamed x1, blocking collectives  59.9 us
    all_gather x1, blocking collectives, shards(): gathered = lax.all_gather(inputs, 'row', axis=0, tiled=True)  40.8 us
    unnamed x8, starting transfers between devices  30.8 us
    all_gather x1, blocking collectives, shards(): dy_rows = lax.all_gather(out_grad, 'col', axis=0, tiled=True)  20 us
  transfers between devices with their start and end apart: 11, of which 3 were waited for; matrix products, arithmetic and copies ran while one was open for 1% of the time, Pallas kernels for 0%

commit v1 on v0

v1 whole, which is shorter than its diff:
```python
import math

import jax
import jax.numpy as jnp
from jax import lax
from jax.experimental import pallas as pl
from jax.experimental.pallas import tpu as pltpu
from jax.sharding import PartitionSpec as P

MESH = pl.DeviceIdType.MESH
BF16 = jnp.bfloat16
F32 = jnp.float32

NZ = 16
NP = 16
TB = 24
TD = 12
TOKENS = 384
W = 464
D2 = 928
COPIES = 240

PLANE = sorted(
    [(a, b) for a in range(4) for b in range(4) if (a, b) != (0, 0)],
    key=lambda o: -(min(o[0], 4 - o[0]) + min(o[1], 4 - o[1])),
)
FAR_FIRST = (2, 1, 3, 0)


def dot(a, b):
    return jnp.dot(a, b, preferred_element_type=F32)


def dot_nt(a, b):
    return lax.dot_general(a, b, (((1,), (1,)), ((), ())), preferred_element_type=F32)


def dot_tn(a, b):
    return lax.dot_general(a, b, (((0,), (0,)), ((), ())), preferred_element_type=F32)


def dense(blocks):
    n, t, w = blocks.shape
    return blocks.astype(F32).reshape(n * t, w).astype(BF16)


def gelu_parts(hidden):
    cdf = 0.5 * (1.0 + lax.erf(hidden / math.sqrt(2.0)))
    pdf = jnp.exp(-0.5 * hidden * hidden) / math.sqrt(2.0 * math.pi)
    return (cdf, pdf)


def unpad(which):
    i = lax.broadcasted_iota(jnp.int32, (4 * TB, 4 * 16), 0)
    j = lax.broadcasted_iota(jnp.int32, (4 * TB, 4 * 16), 1)
    hit = jnp.zeros((4 * TB, 4 * 16), F32)
    for a in range(4):
        low = TB * a + TD * which
        here = (i >= low) & (i < low + TD) & (j == i - low + 16 * a)
        hit = hit + jnp.where(here, 1.0, 0.0)
    return hit.astype(BF16)


def kernel(
    x_ref, dy_ref, wu_hbm, wd_hbm,
    xd_o, dyd_o, hgd_o, act_o, ig_o,
    wu, wu_sib, wd, wd_sib,
    xg, dyb, sa, ra, ah1, ahs, ar2, sb, rb, eg, actb, hgb, sg, gh1, ghs, gr2, igs,
    local_sem, ss, rs,
):
    r, c = lax.axis_index("row"), lax.axis_index("col")
    z, k = r // 2, r % 2
    other = 1 - k
    sign = 1 - 2 * k
    px, py = c // 4, c % 4

    def wrap(v):
        return lax.rem(v + NZ, NZ)

    def zdev(d):
        return {"row": wrap(z + d) * 2 + k, "col": c}

    def pcol(dx, dy):
        return lax.rem(px + dx, 4) * 4 + lax.rem(py + dy, 4)

    def pdev(dx, dy):
        return {"row": r, "col": pcol(dx, dy)}

    sib = {"row": z * 2 + other, "col": c}
    copies = []

    def send(src, dst, dev):
        n = len(copies)
        copy = pltpu.make_async_remote_copy(
            src_ref=src, dst_ref=dst, send_sem=ss.at[n], recv_sem=rs.at[n],
            device_id=dev, device_id_type=MESH,
        )
        copy.start()
        copies.append(copy)
        return copy

    def gather_start(buf):
        return {d: send(buf.at[z], buf.at[z], zdev(d)) for d in (6, -6, 3, -3, 1, -1)}

    def gather_relay(buf, first, d):
        first[d].wait_recv()
        block = wrap(z - d)
        return [send(buf.at[block], buf.at[block], zdev(e)) for e in (1, -1)]

    def gather_far(buf):
        block = wrap(z - 6 * sign)
        return [send(buf.at[block], buf.at[block], zdev(2 * sign))]

    def reduce_start(buf, h1):
        out = []
        for slot, d in enumerate((-2, -5, 4, 7, 1)):
            out.append(send(buf.at[wrap(z + d)], h1.at[slot], zdev(1)))
        for slot, d in enumerate((-4, -7, 2, 5, -1)):
            out.append(send(buf.at[wrap(z + d)], h1.at[5 + slot], zdev(-1)))
        out.append(send(buf.at[wrap(z + 8)], h1.at[10], zdev(-2 * sign)))
        return out

    def reduce_hub(buf, h1, hs, r2, first):
        for copy in first:
            copy.wait_recv()
        far = h1[10].astype(F32)
        second = []
        for slot, d in ((1, -6), (3, 6), (0, -3), (2, 3)):
            total = buf[wrap(z + d)].astype(F32) + h1[slot].astype(F32) + h1[5 + slot].astype(F32)
            if d == -6:
                total = total + jnp.where(k == 0, far, 0.0)
            if d == 6:
                total = total + jnp.where(k == 1, far, 0.0)
            hs[slot] = total.astype(BF16)
            second.append(send(hs.at[slot], r2.at[slot], zdev(d)))
        return second

    def reduce_end(buf, h1, r2, second):
        total = buf[z].astype(F32) + h1[4].astype(F32) + h1[9].astype(F32)
        for copy in second:
            copy.wait_recv()
        for slot in range(4):
            total = total + r2[slot].astype(F32)
        return total

    mine = pl.multiple_of(k * W, 16)
    theirs = pl.multiple_of(other * W, 16)
    load_wd = pltpu.make_async_copy(wd_hbm.at[pl.ds(mine, W)], wd, local_sem.at[0])
    load_wu = pltpu.make_async_copy(wu_hbm, wu, local_sem.at[1])
    load_wd.start()
    load_wu.start()

    dyb[k, c] = dy_ref[...]
    xg[k, z, 0:TD, :] = x_ref[...]
    xg[k, z, TD:16, :] = jnp.zeros((16 - TD, D2), BF16)

    barrier = pltpu.get_barrier_semaphore()
    partners = [pdev(*o) for o in PLANE] + [zdev(d) for d in (6, -6, 3, -3, 2, -2, 1, -1)] + [sib]
    for dev in partners:
        pl.semaphore_signal(barrier, inc=1, device_id=dev, device_id_type=MESH)
    pl.semaphore_wait(barrier, len(partners))

    dy_copies = {o: send(dyb.at[k, c], dyb.at[k, c], pdev(*o)) for o in PLANE}
    x_first = gather_start(xg.at[k])
    to_sib = [send(dyb.at[k, c], dyb.at[k, c], sib)]
    wd_copy = send(wd_hbm.at[pl.ds(theirs, W)], wd_sib, sib)
    wu_copy = send(wu_hbm.at[pl.ds(theirs, W)], wu_sib, sib)

    x_second = gather_relay(xg.at[k], x_first, 3) + gather_relay(xg.at[k], x_first, -3)
    for dx, dy in reversed(PLANE):
        dy_copies[dx, dy].wait_recv()
        block = pcol(4 - dx, 4 - dy)
        to_sib.append(send(dyb.at[k, block], dyb.at[k, block], sib))
    x_second += gather_relay(xg.at[k], x_first, 6) + gather_relay(xg.at[k], x_first, -6)
    x_second += gather_far(xg.at[k])

    load_wd.wait()
    wd_copy.wait_recv()
    for copy in to_sib:
        copy.wait_recv()
    a_copies = {}
    for dx in FAR_FIRST:
        g = lax.rem(px + dx, 4)
        own = dense(dyb[k, pl.ds(4 * g, 4)])
        dyd_o[pl.ds(pl.multiple_of(g * 96, 96), 96), :] = own
        part = dot_nt(own, wd[...]) + dot_nt(dense(dyb[other, pl.ds(4 * g, 4)]), wd_sib[...])
        for i in range(4):
            sa[4 * g + i] = part[TB * i : TB * (i + 1)].astype(BF16)
        for dy in FAR_FIRST:
            if (dx, dy) != (0, 0):
                a_copies[dx, dy] = send(sa.at[pcol(dx, dy)], ra.at[c], pdev(dx, dy))
    ra[c] = sa[c]

    load_wu.wait()
    x_first[1].wait_recv()
    x_first[-1].wait_recv()
    for copy in x_second:
        copy.wait_recv()
    x_sib = send(xg.at[k], xg.at[k], sib)
    x_sib.wait_recv()
    take0, take1 = unpad(0), unpad(1)
    b_copies = {}
    for dx in FAR_FIRST:
        g = lax.rem(px + dx, 4)
        part0 = xg[0, pl.ds(4 * g, 4)].reshape(64, D2)
        part1 = xg[1, pl.ds(4 * g, 4)].reshape(64, D2)
        own = (dot(take0, part0) + dot(take1, part1)).astype(BF16)
        xd_o[pl.ds(pl.multiple_of(g * 96, 96), 96), :] = own
        part = dot(own, wu[...])
        for i in range(4):
            sb[4 * g + i] = part[TB * i : TB * (i + 1)].astype(BF16)
        for dy in FAR_FIRST:
            if (dx, dy) != (0, 0):
                b_copies[dx, dy] = send(sb.at[pcol(dx, dy)], rb.at[c], pdev(dx, dy))
    rb[c] = sb[c]

    for copy in a_copies.values():
        copy.wait_recv()
    a_first = reduce_start(ra, ah1)

    for copy in b_copies.values():
        copy.wait_recv()
    hidden = jnp.zeros((TB, W), F32)
    for i in range(NP):
        hidden = hidden + rb[i].astype(F32)
    cdf, pdf = gelu_parts(hidden)
    eg[z] = (hidden * cdf).astype(BF16)
    slope = cdf + hidden * pdf
    e_first = gather_start(eg)

    a_second = reduce_hub(ra, ah1, ahs, ar2, a_first)
    e_second = []
    for d in (3, -3, 6, -6):
        e_second += gather_relay(eg, e_first, d)
    e_second += gather_far(eg)

    act_grad = reduce_end(ra, ah1, ar2, a_second)
    hgb[k, c] = (act_grad * slope).astype(BF16)
    f_copies = {o: send(hgb.at[k, c], hgb.at[k, c], pdev(*o)) for o in PLANE}
    to_sib = [send(hgb.at[k, c], hgb.at[k, c], sib)]

    e_first[1].wait_recv()
    e_first[-1].wait_recv()
    for copy in e_second:
        copy.wait_recv()
    e_copies = {o: send(eg.at[pcol(*o)], actb.at[k, c], pdev(*o)) for o in PLANE}
    actb[k, c] = eg[c]

    for dx, dy in reversed(PLANE):
        f_copies[dx, dy].wait_recv()
        block = pcol(4 - dx, 4 - dy)
        to_sib.append(send(hgb.at[k, block], hgb.at[k, block], sib))
    wu_copy.wait_recv()
    for copy in to_sib:
        copy.wait_recv()
    for g in range(4):
        own = dense(hgb[k, 4 * g : 4 * g + 4])
        hgd_o[96 * g : 96 * g + 96, :] = own
        part = dot_nt(own, wu[pl.ds(mine, W), :]) + dot_nt(
            dense(hgb[other, 4 * g : 4 * g + 4]), wu_sib[...]
        )
        for i in range(4):
            sg[4 * g + i] = part[TB * i : TB * (i + 1)].astype(BF16)
    g_first = reduce_start(sg, gh1)

    for copy in e_copies.values():
        copy.wait_recv()
    e_sib = send(actb.at[k], actb.at[k], sib)
    g_second = reduce_hub(sg, gh1, ghs, gr2, g_first)
    e_sib.wait_recv()
    for g in range(4):
        for h in range(2):
            act_o[h, 96 * g : 96 * g + 96, :] = dense(actb[h, 4 * g : 4 * g + 4])

    total = reduce_end(sg, gh1, gr2, g_second).astype(BF16)
    i = lax.broadcasted_iota(jnp.int32, (16, TB), 0)
    j = lax.broadcasted_iota(jnp.int32, (16, TB), 1)
    igs[k] = dot(jnp.where(j == i + TD * other, 1.0, 0.0).astype(BF16), total).astype(BF16)
    ig_sib = send(igs.at[k], igs.at[k], sib)
    ig_o[k] = dot(jnp.where(j == i + TD * k, 1.0, 0.0).astype(BF16), total).astype(BF16)
    ig_sib.wait_recv()
    ig_o[other] = igs[other]
    for copy in copies:
        copy.wait_send()


def shards(inputs, out_grad, w_up, w_down):
    vmem = pl.BlockSpec(memory_space=pltpu.VMEM)
    hbm = pl.BlockSpec(memory_space=pl.ANY)

    def blocks(*lead):
        return pltpu.VMEM((*lead, TB, W), BF16)

    xd, dyd, hgd, act, ig = pl.pallas_call(
        kernel,
        name="feed_forward_backward",
        out_shape=[
            jax.ShapeDtypeStruct((TOKENS, D2), BF16),
            jax.ShapeDtypeStruct((TOKENS, W), BF16),
            jax.ShapeDtypeStruct((TOKENS, W), BF16),
            jax.ShapeDtypeStruct((2, TOKENS, W), BF16),
            jax.ShapeDtypeStruct((2, 16, W), BF16),
        ],
        in_specs=[vmem, vmem, hbm, hbm],
        out_specs=[vmem] * 5,
        scratch_shapes=[
            pltpu.VMEM((D2, W), BF16), pltpu.VMEM((W, W), BF16), pltpu.VMEM((W, W), BF16), pltpu.VMEM((W, W), BF16),
            pltpu.VMEM((2, NZ, 16, D2), BF16), blocks(2, NP),
            blocks(NP), blocks(NP), blocks(11), blocks(4), blocks(4),
            blocks(NP), blocks(NP), blocks(NZ), blocks(2, NP), blocks(2, NP),
            blocks(NZ), blocks(11), blocks(4), blocks(4), pltpu.VMEM((2, 16, W), BF16),
            pltpu.SemaphoreType.DMA((2,)), pltpu.SemaphoreType.DMA((COPIES,)), pltpu.SemaphoreType.DMA((COPIES,)),
        ],
        compiler_params=pltpu.CompilerParams(
            collective_id=0, has_side_effects=True, vmem_limit_bytes=48 * 2**20
        ),
    )(inputs, out_grad, w_up, w_down)
    up_grad = dot_tn(xd, hgd)
    down_grad = jnp.concatenate([dot_tn(act[0], dyd), dot_tn(act[1], dyd)], axis=0)
    input_grad = jnp.concatenate([ig[0, :TD], ig[1, :TD]], axis=1)
    return (input_grad, up_grad, down_grad)


def solution(mesh):
    return jax.shard_map(
        shards,
        mesh=mesh,
        in_specs=(P("row", "col"), P("col", "row"), P("col", "row"), P("col", "row")),
        out_specs=(P("row", "col"), P("col", "row"), P("col", "row")),
        check_vma=False,
    )
```

time: 608 us -> 94.1 us (0.15)
  waiting for transfers between devices: 419 us -> 0 us
  blocking collectives: 121 us -> 0 us
  Pallas kernels: 0 us -> 84.3 us
  starting transfers between devices: 30.9 us -> 0 us
  between operations: 14.7 us -> 0.67 us
  matrix products: 10 us -> 2.8 us
    psum x3 -> x0, waiting for transfers between devices: 419 us -> none  [the longest x2 331 us: spread(): return lax.psum(jnp.where(mine, value, jnp.zeros_like(value)), axis)]
    pallas_call x0 -> x1, Pallas kernels: none -> 84.3 us  [shards(): pl.pallas_call(kernel, name='feed_forward_backward', out_shape=[jax.Shape...]
    all_gather x2 -> x0, blocking collectives: 60.8 us -> none  [the longest x1 40.8 us: shards(): gathered = lax.all_gather(inputs, 'row', axis=0, tiled=True)]
    unnamed x1 -> x0, blocking collectives: 59.9 us -> none
    unnamed x8 -> x0, starting transfers between devices: 30.8 us -> none
    dot_general x5 -> x3, matrix products: 10 us -> 2.8 us  [dot_tn(): lax.dot_general(a, b, (((0,), (0,)), ((), ())), preferred_element_type=F32)]
  transfers between devices with their start and end apart: 11 -> 0, of which waited for: 3 -> 0; matrix products, arithmetic and copies ran while one was open for 1% -> 0% of each run, Pallas kernels for 0% -> 0%
where the time goes in v1:
time: 94.1 us; the launch traced here: 93.7 us
  Pallas kernels  84.3 us (90%)
  local copies, waits for them, and re-layouts  3.87 us (4%)
  matrix products  2.8 us (3%)
  other arithmetic  2.11 us (2%)
    pallas_call x1, Pallas kernels, shards(): pl.pallas_call(kernel, name='feed_forward_backward', out_shape=[jax.Shape...  84.3 us
    unnamed x8, local copies, waits for them, and re-layouts  3.87 us
    dot_general x3, matrix products, dot_tn(): lax.dot_general(a, b, (((0,), (0,)), ((), ())), preferred_element_type=F32)  2.8 us

profile of v1, /device:TPU:1, one launch (start us, length us, event | category | flops | bytes accessed | tf_op | source)
XLA Modules:
  0.0 93.7 jit_solution(7547163239653550533)
XLA Ops:
  0.6 0.0 copy-start
  0.6 1.2 %copy-done = bf16[928,464]{1,0:T(8,128)(2,1)S(1)} copy-done((bf16[928,464]{1,0:T(8,128)(2,1)S(1)}, bf16[928,464]{1,0:T(8,128)(2,1)}, u32[]{:S(2)}) %copy-start) | copy-done | bytes 861208
  1.8 0.0 copy-start.1
  1.8 1.2 %copy-done.1 = bf16[928,464]{1,0:T(8,128)(2,1)S(1)} copy-done((bf16[928,464]{1,0:T(8,128)(2,1)S(1)}, bf16[928,464]{1,0:T(8,128)(2,1)}, u32[]{:S(2)}) %copy-start.1) | copy-done | bytes 861208
  3.0 0.0 copy-start.2
  3.0 0.8 copy-done.2
  3.8 0.0 copy-start.3
  3.8 0.7 copy-done.3
  4.5 84.3 %feed_forward_backward.1 = (bf16[384,928]{1,0:T(8,128)(2,1)S(1)}, bf16[384,464]{1,0:T(8,128)(2,1)S(1)}, bf16[384,464]{1,0:T(8,128)(2,1)S(1)}, bf16[2,384,464]{2,1,0:T(8,128)(2,1)S(1)}, bf16[2,16,464]{2,1,0:T(8,128)(2,1)S(1)}) custom-call(bf16[12,928]{1,0:T(8,128)(2,1)S(1)} %copy-done.2, bf16[24,464]{1,0:T(8,128)(2,1)S(1)} %copy-done.3, ...), custom_call_target="tpu_custom_call" | custom-call | tf_op jit(solution)/shard_map/feed_forward_backward/pallas_call | solution.py:294
  88.8 0.7 pad_maximum_fusion.1
  89.5 0.4 fusion
  89.9 0.4 fusion.2
  90.4 1.4 %pad_maximum_fusion = f32[928,464]{1,0:T(8,128)} fusion(f32[464,464]{1,0:T(8,128)S(1)} %fusion, f32[464,464]{1,0:T(8,128)S(1)} %fusion.2), kind=kLoop, calls=%fused_computation | loop fusion | flops 430592 | bytes 3444736 | tf_op jit(solution)/shard_map/concatenate | solution.py:319
  91.8 1.9 %fusion.6 = f32[928,464]{1,0:T(8,128)} fusion(bf16[384,928]{1,0:T(8,128)(2,1)S(1)} %get-tuple-element.9, bf16[384,464]{1,0:T(8,128)(2,1)S(1)} %get-tuple-element.10), kind=kOutput, calls=%fused_computation.10 | convolution fusion | flops 330694656 | bytes 2791424 | tf_op jit(solution)/shard_map/dot_general | solution.py:39
  (1 shorter events, 0.0 us)
Async XLA Ops:
  0.6 1.2 %copy-start = (bf16[928,464]{1,0:T(8,128)(2,1)S(1)}, bf16[928,464]{1,0:T(8,128)(2,1)}, u32[]{:S(2)}) copy-start(bf16[928,464]{1,0:T(8,128)(2,1)} %wu_hbm.1) | copy-start | bytes 2583556
  1.8 1.2 %copy-start.1 = (bf16[928,464]{1,0:T(8,128)(2,1)S(1)}, bf16[928,464]{1,0:T(8,128)(2,1)}, u32[]{:S(2)}) copy-start(bf16[928,464]{1,0:T(8,128)(2,1)} %wd_hbm.1) | copy-start | bytes 2583556
  3.0 0.8 copy-start.2
  3.8 0.7 copy-start.3

commit v2 on v1

v2 whole, which is shorter than its diff:
```python
import math

import jax
import jax.numpy as jnp
from jax import lax
from jax.experimental import pallas as pl
from jax.experimental.pallas import tpu as pltpu
from jax.sharding import PartitionSpec as P

MESH = pl.DeviceIdType.MESH
BF16 = jnp.bfloat16
F32 = jnp.float32

NZ = 16
NP = 16
TB = 24
TD = 12
TOKENS = 384
W = 464
D2 = 928
COPIES = 240

PLANE = sorted(
    [(a, b) for a in range(4) for b in range(4) if (a, b) != (0, 0)],
    key=lambda o: -(min(o[0], 4 - o[0]) + min(o[1], 4 - o[1])),
)
FAR_FIRST = (2, 1, 3, 0)
NEAR_FIRST = (0, 1, 3, 2)
SLOTS = {
    -2: (0, 1), -5: (1, 1), 4: (2, 1), 7: (3, 1), 1: (4, 1),
    -4: (5, -1), -7: (6, -1), 2: (7, -1), 5: (8, -1), -1: (9, -1), 8: (10, 0),
}
ARRIVAL = ((0, 1, -1, 3), (-3, 2, -2, 4), (-4, 6, -6, 5), (-5, 7, -7, 8))


def dot(a, b):
    return jnp.dot(a, b, preferred_element_type=F32)


def dot_nt(a, b):
    return lax.dot_general(a, b, (((1,), (1,)), ((), ())), preferred_element_type=F32)


def dot_tn(a, b):
    return lax.dot_general(a, b, (((0,), (0,)), ((), ())), preferred_element_type=F32)


def dense(blocks):
    n, t, w = blocks.shape
    return blocks.astype(F32).reshape(n * t, w).astype(BF16)


def gelu_parts(hidden):
    cdf = 0.5 * (1.0 + lax.erf(hidden / math.sqrt(2.0)))
    pdf = jnp.exp(-0.5 * hidden * hidden) / math.sqrt(2.0 * math.pi)
    return (cdf, pdf)


def stack(blocks):
    return jnp.concatenate([block.astype(F32) for block in blocks], axis=0).astype(BF16)


def kernel(
    x_hbm, dy_hbm, wu_hbm, wd_hbm,
    xd_hbm, dyd_hbm, hgd_hbm, act_hbm, input_grad,
    act, wu, wu_sib, wd, wd_sib,
    xg, xd, dyd, hgd, dyb, sa, ra, ah1, ahs, ar2, sb, rb, eg, actb, hgb, sg, sgf, gh1, ghs, gr2, igs,
    local_sem, ss, rs, bss, brs,
):
    r, c = lax.axis_index("row"), lax.axis_index("col")
    z, k = r // 2, r % 2
    other = 1 - k
    sign = 1 - 2 * k
    px, py = c // 4, c % 4

    def wrap(v):
        return lax.rem(v + NZ, NZ)

    def zdev(d):
        return {"row": wrap(z + d) * 2 + k, "col": c}

    def pcol(dx, dy):
        return lax.rem(px + dx, 4) * 4 + lax.rem(py + dy, 4)

    def pdev(dx, dy):
        return {"row": r, "col": pcol(dx, dy)}

    sib = {"row": z * 2 + other, "col": c}
    copies = []

    def send(src, dst, dev):
        n = len(copies)
        copy = pltpu.make_async_remote_copy(
            src_ref=src, dst_ref=dst, send_sem=ss.at[n], recv_sem=rs.at[n],
            device_id=dev, device_id_type=MESH,
        )
        copy.start()
        copies.append(copy)
        return copy

    def gather_start(buf):
        return {-d: send(buf.at[z], buf.at[z], zdev(d)) for d in (6, -6, 3, -3, 1, -1)}

    def gather_relay(buf, got, d):
        got[d].wait_recv()
        block = wrap(z + d)
        for e in (1, -1):
            got[d - e] = send(buf.at[block], buf.at[block], zdev(e))

    def gather_far(buf, got):
        block = wrap(z - 6 * sign)
        got[8] = send(buf.at[block], buf.at[block], zdev(2 * sign))

    def reduce_start(buf, h1, ds=(8, -5, 7, -7, 5, -2, 4, -4, 2, 1, -1)):
        out = {}
        for d in ds:
            if d in SLOTS:
                slot, e = SLOTS[d]
                out[slot] = send(buf.at[wrap(z + d)], h1.at[slot], zdev(-2 * sign if d == 8 else e))
        return out

    def reduce_hub(buf, h1, hs, r2, first):
        first[10].wait_recv()
        far = h1[10].astype(F32)
        second = []
        for slot, d in ((1, -6), (3, 6), (0, -3), (2, 3)):
            first[slot].wait_recv()
            first[5 + slot].wait_recv()
            total = buf[wrap(z + d)].astype(F32) + h1[slot].astype(F32) + h1[5 + slot].astype(F32)
            if d == -6:
                total = total + jnp.where(k == 0, far, 0.0)
            if d == 6:
                total = total + jnp.where(k == 1, far, 0.0)
            hs[slot] = total.astype(BF16)
            second.append(send(hs.at[slot], r2.at[slot], zdev(d)))
        return second

    def reduce_end(buf, h1, r2, first, second):
        first[4].wait_recv()
        first[9].wait_recv()
        total = buf[z].astype(F32) + h1[4].astype(F32) + h1[9].astype(F32)
        for copy in second:
            copy.wait_recv()
        for slot in range(4):
            total = total + r2[slot].astype(F32)
        return total

    mine = pl.multiple_of(k * W, 16)
    theirs = pl.multiple_of(other * W, 16)
    load_x = pltpu.make_async_copy(x_hbm, xg.at[k, z], local_sem.at[0])
    load_dy = pltpu.make_async_copy(dy_hbm, dyb.at[k, c], local_sem.at[1])
    load_wd = pltpu.make_async_copy(wd_hbm.at[pl.ds(mine, W)], wd, local_sem.at[2])
    load_wu = pltpu.make_async_copy(wu_hbm, wu, local_sem.at[3])
    load_x.start()
    load_dy.start()
    load_wd.start()
    load_wu.start()

    barrier = pltpu.get_barrier_semaphore()
    partners = [pdev(*o) for o in PLANE] + [zdev(d) for d in (6, -6, 3, -3, 2, -2, 1, -1)] + [sib]
    for dev in partners:
        pl.semaphore_signal(barrier, inc=1, device_id=dev, device_id_type=MESH)
    load_x.wait()
    load_dy.wait()
    pl.semaphore_wait(barrier, len(partners))

    dy_copies = {o: send(dyb.at[k, c], dyb.at[k, c], pdev(*o)) for o in PLANE}
    x_got = gather_start(xg.at[k])
    to_sib = {0: [send(dyb.at[k, c], dyb.at[k, c], sib)], 1: [], 2: [], 3: []}
    x_sib = {0: send(xg.at[k, z], xg.at[k, z], sib)}
    wd_copy = send(wd_hbm.at[pl.ds(theirs, W)], wd_sib, sib)
    wu_copy = send(wu_hbm.at[pl.ds(theirs, W)], wu_sib, sib)

    a_copies = {}

    def forward(dx):
        for dy in NEAR_FIRST:
            if (dx, dy) != (0, 0):
                dy_copies[dx, dy].wait_recv()
                block = pcol(4 - dx, 4 - dy)
                to_sib[dx].append(send(dyb.at[k, block], dyb.at[k, block], sib))

    def act_part(dx):
        for copy in to_sib[dx]:
            copy.wait_recv()
        g = lax.rem(px + 4 - dx, 4)
        own = dense(dyb[k, pl.ds(4 * g, 4)])
        dyd[pl.ds(pl.multiple_of(g * 96, 96), 96), :] = own
        part = dot_nt(own, wd[...]) + dot_nt(dense(dyb[other, pl.ds(4 * g, 4)]), wd_sib[...])
        for i in range(4):
            sa[4 * g + i] = part[TB * i : TB * (i + 1)].astype(BF16)
        for dy in FAR_FIRST:
            if (dx, dy) != (0, 0):
                to = (4 - dx) % 4, dy
                a_copies[to] = send(sa.at[pcol(*to)], ra.at[c], pdev(*to))

    b_copies = []

    def x_forward(*ds):
        for d in ds:
            if d not in (3, -3, 6, -6):
                x_got[d].wait_recv()
            block = wrap(z + d)
            x_sib[d] = send(xg.at[k, block], xg.at[k, block], sib)

    def hidden_part(n):
        for d in ARRIVAL[n]:
            x_sib[d].wait_recv()
        blocks = [wrap(z + d) for d in ARRIVAL[n]]
        own = stack([xg[core, block] for block in blocks for core in range(2)])
        xd[96 * n : 96 * n + 96, :] = own
        part = dot(own, wu[...])
        for i, block in enumerate(blocks):
            sb[block] = part[TB * i : TB * (i + 1)].astype(BF16)
        for i, block in enumerate(blocks):
            there = pltpu.make_async_remote_copy(
                src_ref=sb.at[block], dst_ref=rb.at[c], send_sem=bss.at[4 * n + i], recv_sem=brs.at[c],
                device_id={"row": r, "col": block}, device_id_type=MESH,
            )
            here = pltpu.make_async_copy(sb.at[block], rb.at[c], brs.at[c])
            pl.when(block != c)(there.start)
            pl.when(block == c)(here.start)
            b_copies.append((block, there))

    forward(0)
    x_forward(1, -1)
    gather_relay(xg.at[k], x_got, 3)
    gather_relay(xg.at[k], x_got, -3)
    forward(1)
    load_wd.wait()
    wd_copy.wait_recv()
    act_part(0)
    forward(3)
    act_part(1)
    x_forward(3, -3)
    forward(2)
    act_part(3)
    gather_relay(xg.at[k], x_got, 6)
    gather_relay(xg.at[k], x_got, -6)
    gather_far(xg.at[k], x_got)
    act_part(2)
    ra[c] = sa[c]
    x_forward(2, -2, 4, -4, 6, -6)
    load_wu.wait()
    hidden_part(0)
    hidden_part(1)
    x_forward(5, -5, 7, -7, 8)
    hidden_part(2)
    hidden_part(3)

    for copy in a_copies.values():
        copy.wait_recv()
    a_first = reduce_start(ra, ah1)
    a_second = reduce_hub(ra, ah1, ahs, ar2, a_first)

    for j in range(NP):
        pltpu.make_async_remote_copy(
            src_ref=sb.at[j], dst_ref=rb.at[j], send_sem=bss.at[j], recv_sem=brs.at[j],
            device_id=sib, device_id_type=MESH,
        ).wait_recv()
    hidden = jnp.zeros((TB, W), F32)
    for i in range(NP):
        hidden = hidden + rb[i].astype(F32)
    cdf, pdf = gelu_parts(hidden)
    eg[z] = (hidden * cdf).astype(BF16)
    slope = cdf + hidden * pdf

    act_grad = reduce_end(ra, ah1, ar2, a_first, a_second)
    hgb[k, c] = (act_grad * slope).astype(BF16)
    f_copies = {o: send(hgb.at[k, c], hgb.at[k, c], pdev(*o)) for o in PLANE}
    f_sib = [send(hgb.at[k, c], hgb.at[k, c], sib)]
    e_got = gather_start(eg)

    def f_forward(offsets):
        for dx, dy in offsets:
            f_copies[dx, dy].wait_recv()
            block = pcol(4 - dx, 4 - dy)
            f_sib.append(send(hgb.at[k, block], hgb.at[k, block], sib))

    f_forward(PLANE[:4:-1])
    gather_relay(eg, e_got, 3)
    gather_relay(eg, e_got, -3)
    f_forward(PLANE[4::-1])
    wu_copy.wait_recv()
    for copy in f_sib:
        copy.wait_recv()
    g_first = {}
    for n in (3, 2, 1, 0):
        blocks = [wrap(z + d) for d in ARRIVAL[n]]
        own = stack([hgb[k, block] for block in blocks])
        hgd[96 * n : 96 * n + 96, :] = own
        part = dot_nt(own, wu[pl.ds(mine, W), :]) + dot_nt(
            stack([hgb[other, block] for block in blocks]), wu_sib[...]
        )
        for i, block in enumerate(blocks):
            sgf[block] = part[TB * i : TB * (i + 1)]
            sg[block] = part[TB * i : TB * (i + 1)].astype(BF16)
        g_first |= reduce_start(sg, gh1, ARRIVAL[n])
        if n == 3:
            gather_relay(eg, e_got, 6)
            gather_relay(eg, e_got, -6)
            gather_far(eg, e_got)

    g_second = reduce_hub(sgf, gh1, ghs, gr2, g_first)
    for d in (1, -1, 2, -2, 4, -4, 5, -5, 7, -7, 8):
        e_got[d].wait_recv()
    e_copies = [send(eg.at[pcol(*o)], actb.at[k, c], pdev(*o)) for o in PLANE]
    actb[k, c] = eg[c]

    flush = [pltpu.make_async_copy(xd, xd_hbm, local_sem.at[4])]
    flush.append(pltpu.make_async_copy(hgd, hgd_hbm, local_sem.at[5]))
    flush.append(pltpu.make_async_copy(dyd, dyd_hbm, local_sem.at[6]))
    for copy in flush:
        copy.start()
    for copy in e_copies:
        copy.wait_recv()
    e_sib = send(actb.at[k], actb.at[k], sib)
    act[k] = dense(actb[k])
    e_sib.wait_recv()
    act[other] = dense(actb[other])
    flush.append(pltpu.make_async_copy(act, act_hbm, local_sem.at[7]))
    flush[3].start()

    total = reduce_end(sgf, gh1, gr2, g_first, g_second).astype(BF16)
    i = lax.broadcasted_iota(jnp.int32, (16, TB), 0)
    j = lax.broadcasted_iota(jnp.int32, (16, TB), 1)
    igs[k] = dot(jnp.where(j == i + TD * other, 1.0, 0.0).astype(BF16), total).astype(BF16)
    ig_sib = send(igs.at[k], igs.at[k], sib)
    kept = dot(jnp.where(j == i + TD * k, 1.0, 0.0).astype(BF16), total)
    ig_sib.wait_recv()
    came = igs[other].astype(F32)
    halves = [jnp.where(k == 0, kept, came), jnp.where(k == 0, came, kept)]
    input_grad[...] = jnp.concatenate(halves, axis=1)[:TD].astype(BF16)
    for copy in flush:
        copy.wait()
    for copy in copies:
        copy.wait_send()
    for block, there in b_copies:
        pl.when(block != c)(there.wait_send)


def products(
    xd_hbm, dyd_hbm, hgd_hbm, act_hbm, ig_hbm, ig_out, up_hbm, down_hbm,
    xd, dyd, hgd, act, ig, up, down, load_sems, sems,
):
    pairs = ((ig_hbm, ig), (xd_hbm, xd), (hgd_hbm, hgd), (act_hbm, act), (dyd_hbm, dyd))
    loads = [pltpu.make_async_copy(a, b, load_sems.at[n]) for n, (a, b) in enumerate(pairs)]
    for load in loads:
        load.start()
    copies = []

    def write(src, dst):
        copies.append(pltpu.make_async_copy(src, dst, sems.at[len(copies)]))
        copies[-1].start()

    loads[0].wait()
    write(ig, ig_out)
    loads[1].wait()
    loads[2].wait()
    for low, high in ((0, 512), (512, D2)):
        up[low:high, :] = dot_tn(xd[:, low:high], hgd[...])
        write(up.at[low:high], up_hbm.at[low:high])
    loads[3].wait()
    loads[4].wait()
    for n in range(2):
        down[n * W : n * W + W, :] = dot_tn(act[n], dyd[...])
        write(down.at[n * W : n * W + W], down_hbm.at[n * W : n * W + W])
    for copy in copies:
        copy.wait()


def shards(inputs, out_grad, w_up, w_down):
    vmem = pl.BlockSpec(memory_space=pltpu.VMEM)
    hbm = pl.BlockSpec(memory_space=pltpu.HBM)

    def blocks(*lead):
        return pltpu.VMEM((*lead, TB, W), BF16)

    gathered = pl.pallas_call(
        kernel,
        name="feed_forward_backward",
        out_shape=[
            jax.ShapeDtypeStruct((TOKENS, D2), BF16),
            jax.ShapeDtypeStruct((TOKENS, W), BF16),
            jax.ShapeDtypeStruct((TOKENS, W), BF16),
            jax.ShapeDtypeStruct((2, TOKENS, W), BF16),
            jax.ShapeDtypeStruct((TD, D2), BF16),
        ],
        in_specs=[hbm] * 4,
        out_specs=[hbm] * 4 + [vmem],
        scratch_shapes=[
            pltpu.VMEM((2, TOKENS, W), BF16), pltpu.VMEM((D2, W), BF16), pltpu.VMEM((W, W), BF16), pltpu.VMEM((W, W), BF16), pltpu.VMEM((W, W), BF16),
            pltpu.VMEM((2, NZ, TD, D2), BF16), pltpu.VMEM((TOKENS, D2), BF16),
            pltpu.VMEM((TOKENS, W), BF16), pltpu.VMEM((TOKENS, W), BF16), blocks(2, NP),
            blocks(NP), blocks(NP), blocks(11), blocks(4), blocks(4),
            blocks(NP), blocks(NP), blocks(NZ), blocks(2, NP), blocks(2, NP),
            blocks(NZ), pltpu.VMEM((NZ, TB, W), F32), blocks(11), blocks(4), blocks(4),
            pltpu.VMEM((2, 16, W), BF16),
            pltpu.SemaphoreType.DMA((8,)), pltpu.SemaphoreType.DMA((COPIES,)), pltpu.SemaphoreType.DMA((COPIES,)),
            pltpu.SemaphoreType.DMA((NP,)), pltpu.SemaphoreType.DMA((NP,)),
        ],
        compiler_params=pltpu.CompilerParams(
            collective_id=0, has_side_effects=True, vmem_limit_bytes=60 * 2**20
        ),
    )(inputs, out_grad, w_up, w_down)
    return pl.pallas_call(
        products,
        name="weight_gradients",
        out_shape=[
            jax.ShapeDtypeStruct((TD, D2), BF16),
            jax.ShapeDtypeStruct((D2, W), F32),
            jax.ShapeDtypeStruct((D2, W), F32),
        ],
        in_specs=[hbm] * 5,
        out_specs=[hbm] * 3,
        scratch_shapes=[
            pltpu.VMEM((TOKENS, D2), BF16), pltpu.VMEM((TOKENS, W), BF16), pltpu.VMEM((TOKENS, W), BF16),
            pltpu.VMEM((2, TOKENS, W), BF16), pltpu.VMEM((TD, D2), BF16),
            pltpu.VMEM((D2, W), F32), pltpu.VMEM((D2, W), F32),
            pltpu.SemaphoreType.DMA((5,)), pltpu.SemaphoreType.DMA((5,)),
        ],
        compiler_params=pltpu.CompilerParams(vmem_limit_bytes=60 * 2**20),
    )(*gathered)


def solution(mesh):
    return jax.shard_map(
        shards,
        mesh=mesh,
        in_specs=(P("row", "col"), P("col", "row"), P("col", "row"), P("col", "row")),
        out_specs=(P("row", "col"), P("col", "row"), P("col", "row")),
        check_vma=False,
    )
```

time: 94.1 us -> 82.2 us (0.87)
  local copies, waits for them, and re-layouts: 3.87 us -> 0 us
  Pallas kernels: 84.3 us -> 81.4 us
  matrix products: 2.8 us -> 0 us
  other arithmetic: 2.11 us -> 0 us
    pallas_call x1, Pallas kernels: 84.3 us -> 77.7 us  [shards(): pl.pallas_call(kernel, name='feed_forward_backward', out_shape=[jax.Shape...]
    unnamed x8 -> x0, local copies, waits for them, and re-layouts: 3.87 us -> none
    pallas_call x0 -> x1, Pallas kernels: none -> 3.72 us  [shards(): pl.pallas_call(products, name='weight_gradients', out_shape=[jax.ShapeDty...]
    dot_general x3 -> x0, matrix products: 2.8 us -> none  [dot_tn(): lax.dot_general(a, b, (((0,), (0,)), ((), ())), preferred_element_type=F32)]
    concatenate x2 -> x0, other arithmetic: 2.11 us -> none  [the longest x1 1.41 us: shards(): jnp.concatenate([dot_tn(act[0], dyd), dot_tn(act[1], dyd)], axis=0)]
where the time goes in v2:
time: 82.2 us; the launch traced here: 82 us
  Pallas kernels  81.4 us (99%)
    pallas_call x1, Pallas kernels, shards(): pl.pallas_call(kernel, name='feed_forward_backward', out_shape=[jax.Shape...  77.7 us
    pallas_call x1, Pallas kernels, shards(): pl.pallas_call(products, name='weight_gradients', out_shape=[jax.ShapeDty...  3.72 us

profile of v2, /device:TPU:1, one launch (start us, length us, event | category | flops | bytes accessed | tf_op | source)
XLA Modules:
  0.0 82.0 jit_solution(12483628366639110611)
XLA Ops:
  0.6 77.7 %feed_forward_backward.1 = (bf16[384,928]{1,0:T(8,128)(2,1)}, bf16[384,464]{1,0:T(8,128)(2,1)}, bf16[384,464]{1,0:T(8,128)(2,1)}, bf16[2,384,464]{2,1,0:T(8,128)(2,1)}, bf16[12,928]{1,0:T(8,128)(2,1)}) custom-call(bf16[12,928]{1,0:T(8,128)(2,1)} %x_hbm.1, bf16[24,464]{1,0:T(8,128)(2,1)} %dy_hbm.1, bf16[928,464]{1,0:T(8,128)(2,1)} %wu_hbm.1, ...), custom_call_target="tpu_custom_call" | custom-call | tf_op jit(solution)/shard_map/feed_forward_backward/pallas_call | solution.py:379
  78.3 3.7 %weight_gradients.1 = (bf16[12,928]{1,0:T(8,128)(2,1)}, f32[928,464]{1,0:T(8,128)}, f32[928,464]{1,0:T(8,128)}) custom-call(bf16[384,928]{1,0:T(8,128)(2,1)} %get-tuple-element.8.xd_hbm, bf16[384,464]{1,0:T(8,128)(2,1)} %get-tuple-element.9.dyd_hbm, bf16[384,464]{1,0:T(8,128)(2,1)} %get-tuple-element.10.hgd_hbm, ...), custom_call_target="tpu_custom_call" | custom-call | tf_op jit(solution)/shard_map/weight_gradients/pallas_call | solution.py:406

commit v3 on v2

--- a/solution.py
+++ b/solution.py
@@ -41,10 +41,6 @@
     return lax.dot_general(a, b, (((1,), (1,)), ((), ())), preferred_element_type=F32)
 
 
-def dot_tn(a, b):
-    return lax.dot_general(a, b, (((0,), (0,)), ((), ())), preferred_element_type=F32)
-
-
 def dense(blocks):
     n, t, w = blocks.shape
     return blocks.astype(F32).reshape(n * t, w).astype(BF16)
@@ -63,9 +59,9 @@
 def kernel(
     x_hbm, dy_hbm, wu_hbm, wd_hbm,
     xd_hbm, dyd_hbm, hgd_hbm, act_hbm, input_grad,
-    act, wu, wu_sib, wd, wd_sib,
+    act, xdt, wu, wu_sib, wd, wd_sib,
     xg, xd, dyd, hgd, dyb, sa, ra, ah1, ahs, ar2, sb, rb, eg, actb, hgb, sg, sgf, gh1, ghs, gr2, igs,
-    local_sem, ss, rs, bss, brs,
+    local_sem, ss, rs, bss, brs, ess, ers, ass, ars,
 ):
     r, c = lax.axis_index("row"), lax.axis_index("col")
     z, k = r // 2, r % 2
@@ -97,6 +93,25 @@
         copy.start()
         copies.append(copy)
         return copy
+
+    maybe = []
+
+    def send_column(src, dst, col, sends, n, recvs):
+        there = pltpu.make_async_remote_copy(
+            src_ref=src, dst_ref=dst.at[c], send_sem=sends.at[n], recv_sem=recvs.at[c],
+            device_id={"row": r, "col": col}, device_id_type=MESH,
+        )
+        here = pltpu.make_async_copy(src, dst.at[c], recvs.at[c])
+        pl.when(col != c)(there.start)
+        pl.when(col == c)(here.start)
+        maybe.append((col != c, there))
+
+    def wait_columns(dst, sends, recvs):
+        for j in range(NP):
+            pltpu.make_async_remote_copy(
+                src_ref=dst.at[j], dst_ref=dst.at[j], send_sem=sends.at[j], recv_sem=recvs.at[j],
+                device_id=sib, device_id_type=MESH,
+            ).wait_recv()
 
     def gather_start(buf):
         return {-d: send(buf.at[z], buf.at[z], zdev(d)) for d in (6, -6, 3, -3, 1, -1)}
@@ -157,15 +172,15 @@
     load_wu.start()
 
     barrier = pltpu.get_barrier_semaphore()
-    partners = [pdev(*o) for o in PLANE] + [zdev(d) for d in (6, -6, 3, -3, 2, -2, 1, -1)] + [sib]
+    partners = [zdev(d) for d in (6, -6)] + [pdev(*o) for o in PLANE] + [zdev(d) for d in (3, -3, 2, -2, 1, -1)] + [sib]
     for dev in partners:
         pl.semaphore_signal(barrier, inc=1, device_id=dev, device_id_type=MESH)
     load_x.wait()
     load_dy.wait()
     pl.semaphore_wait(barrier, len(partners))
 
+    x_got = gather_start(xg.at[k])
     dy_copies = {o: send(dyb.at[k, c], dyb.at[k, c], pdev(*o)) for o in PLANE}
-    x_got = gather_start(xg.at[k])
     to_sib = {0: [send(dyb.at[k, c], dyb.at[k, c], sib)], 1: [], 2: [], 3: []}
     x_sib = {0: send(xg.at[k, z], xg.at[k, z], sib)}
     wd_copy = send(wd_hbm.at[pl.ds(theirs, W)], wd_sib, sib)
@@ -194,7 +209,6 @@
                 to = (4 - dx) % 4, dy
                 a_copies[to] = send(sa.at[pcol(*to)], ra.at[c], pdev(*to))
 
-    b_copies = []
 
     def x_forward(*ds):
         for d in ds:
@@ -213,14 +227,7 @@
         for i, block in enumerate(blocks):
             sb[block] = part[TB * i : TB * (i + 1)].astype(BF16)
         for i, block in enumerate(blocks):
-            there = pltpu.make_async_remote_copy(
-                src_ref=sb.at[block], dst_ref=rb.at[c], send_sem=bss.at[4 * n + i], recv_sem=brs.at[c],
-                device_id={"row": r, "col": block}, device_id_type=MESH,
-            )
-            here = pltpu.make_async_copy(sb.at[block], rb.at[c], brs.at[c])
-            pl.when(block != c)(there.start)
-            pl.when(block == c)(here.start)
-            b_copies.append((block, there))
+            send_column(sb.at[block], rb, block, bss, 4 * n + i, brs)
 
     forward(0)
     x_forward(1, -1)
@@ -234,10 +241,10 @@
     act_part(1)
     x_forward(3, -3)
     forward(2)
-    act_part(3)
     gather_relay(xg.at[k], x_got, 6)
     gather_relay(xg.at[k], x_got, -6)
     gather_far(xg.at[k], x_got)
+    act_part(3)
     act_part(2)
     ra[c] = sa[c]
     x_forward(2, -2, 4, -4, 6, -6)
@@ -248,16 +255,24 @@
     hidden_part(2)
     hidden_part(3)
 
-    for copy in a_copies.values():
-        copy.wait_recv()
-    a_first = reduce_start(ra, ah1)
+    a_first = {}
+    for d, (slot, e) in SLOTS.items():
+        a_first[slot] = pltpu.make_async_remote_copy(
+            src_ref=ra.at[wrap(z + d)], dst_ref=ah1.at[slot], send_sem=ass.at[slot], recv_sem=ars.at[slot],
+            device_id=zdev(-2 * sign if d == 8 else e), device_id_type=MESH,
+        )
+
+    def pass_on(block):
+        for d, (slot, _) in SLOTS.items():
+            pl.when(block == wrap(z + d))(a_first[slot].start)
+
+    pass_on(c)
+    for dx, dy in reversed(PLANE):
+        a_copies[dx, dy].wait_recv()
+        pass_on(pcol(4 - dx, 4 - dy))
     a_second = reduce_hub(ra, ah1, ahs, ar2, a_first)
 
-    for j in range(NP):
-        pltpu.make_async_remote_copy(
-            src_ref=sb.at[j], dst_ref=rb.at[j], send_sem=bss.at[j], recv_sem=brs.at[j],
-            device_id=sib, device_id_type=MESH,
-        ).wait_recv()
+    wait_columns(rb, bss, brs)
     hidden = jnp.zeros((TB, W), F32)
     for i in range(NP):
         hidden = hidden + rb[i].astype(F32)
@@ -271,16 +286,22 @@
     f_sib = [send(hgb.at[k, c], hgb.at[k, c], sib)]
     e_got = gather_start(eg)
 
+    def e_send(*ds):
+        for d in ds:
+            if d not in (0, 3, -3, 6, -6):
+                e_got[d].wait_recv()
+            block = wrap(z + d)
+            send_column(eg.at[block], actb.at[k], block, ess, d + 7, ers)
+
     def f_forward(offsets):
         for dx, dy in offsets:
             f_copies[dx, dy].wait_recv()
             block = pcol(4 - dx, 4 - dy)
             f_sib.append(send(hgb.at[k, block], hgb.at[k, block], sib))
 
-    f_forward(PLANE[:4:-1])
+    f_forward(reversed(PLANE))
     gather_relay(eg, e_got, 3)
     gather_relay(eg, e_got, -3)
-    f_forward(PLANE[4::-1])
     wu_copy.wait_recv()
     for copy in f_sib:
         copy.wait_recv()
@@ -300,24 +321,23 @@
             gather_relay(eg, e_got, 6)
             gather_relay(eg, e_got, -6)
             gather_far(eg, e_got)
+        if n == 2:
+            e_send(0, 3, -3, 6, -6, 1, -1)
+    e_send(2, -2, 4, -4)
 
     g_second = reduce_hub(sgf, gh1, ghs, gr2, g_first)
-    for d in (1, -1, 2, -2, 4, -4, 5, -5, 7, -7, 8):
-        e_got[d].wait_recv()
-    e_copies = [send(eg.at[pcol(*o)], actb.at[k, c], pdev(*o)) for o in PLANE]
-    actb[k, c] = eg[c]
-
-    flush = [pltpu.make_async_copy(xd, xd_hbm, local_sem.at[4])]
+    e_send(5, -5, 7, -7, 8)
+    xdt[...] = xd[...].T
+    flush = [pltpu.make_async_copy(xdt, xd_hbm, local_sem.at[4])]
     flush.append(pltpu.make_async_copy(hgd, hgd_hbm, local_sem.at[5]))
     flush.append(pltpu.make_async_copy(dyd, dyd_hbm, local_sem.at[6]))
     for copy in flush:
         copy.start()
-    for copy in e_copies:
-        copy.wait_recv()
+    wait_columns(actb.at[k], ess, ers)
     e_sib = send(actb.at[k], actb.at[k], sib)
-    act[k] = dense(actb[k])
+    act[pl.ds(mine, W), :] = dense(actb[k]).T
     e_sib.wait_recv()
-    act[other] = dense(actb[other])
+    act[pl.ds(theirs, W), :] = dense(actb[other]).T
     flush.append(pltpu.make_async_copy(act, act_hbm, local_sem.at[7]))
     flush[3].start()
 
@@ -333,10 +353,10 @@
     input_grad[...] = jnp.concatenate(halves, axis=1)[:TD].astype(BF16)
     for copy in flush:
         copy.wait()
-    for copy in copies:
+    for copy in [*copies, *a_first.values()]:
         copy.wait_send()
-    for block, there in b_copies:
-        pl.when(block != c)(there.wait_send)
+    for sent, there in maybe:
+        pl.when(sent)(there.wait_send)
 
 
 def products(
@@ -358,12 +378,12 @@
     loads[1].wait()
     loads[2].wait()
     for low, high in ((0, 512), (512, D2)):
-        up[low:high, :] = dot_tn(xd[:, low:high], hgd[...])
+        up[low:high, :] = dot(xd[low:high, :], hgd[...])
         write(up.at[low:high], up_hbm.at[low:high])
     loads[3].wait()
     loads[4].wait()
     for n in range(2):
-        down[n * W : n * W + W, :] = dot_tn(act[n], dyd[...])
+        down[n * W : n * W + W, :] = dot(act[n * W : n * W + W, :], dyd[...])
         write(down.at[n * W : n * W + W], down_hbm.at[n * W : n * W + W])
     for copy in copies:
         copy.wait()
@@ -380,16 +400,16 @@
         kernel,
         name="feed_forward_backward",
         out_shape=[
-            jax.ShapeDtypeStruct((TOKENS, D2), BF16),
+            jax.ShapeDtypeStruct((D2, TOKENS), BF16),
             jax.ShapeDtypeStruct((TOKENS, W), BF16),
             jax.ShapeDtypeStruct((TOKENS, W), BF16),
-            jax.ShapeDtypeStruct((2, TOKENS, W), BF16),
+            jax.ShapeDtypeStruct((D2, TOKENS), BF16),
             jax.ShapeDtypeStruct((TD, D2), BF16),
         ],
         in_specs=[hbm] * 4,
         out_specs=[hbm] * 4 + [vmem],
         scratch_shapes=[
-            pltpu.VMEM((2, TOKENS, W), BF16), pltpu.VMEM((D2, W), BF16), pltpu.VMEM((W, W), BF16), pltpu.VMEM((W, W), BF16), pltpu.VMEM((W, W), BF16),
+            pltpu.VMEM((D2, TOKENS), BF16), pltpu.VMEM((D2, TOKENS), BF16), pltpu.VMEM((D2, W), BF16), pltpu.VMEM((W, W), BF16), pltpu.VMEM((W, W), BF16), pltpu.VMEM((W, W), BF16),
             pltpu.VMEM((2, NZ, TD, D2), BF16), pltpu.VMEM((TOKENS, D2), BF16),
             pltpu.VMEM((TOKENS, W), BF16), pltpu.VMEM((TOKENS, W), BF16), blocks(2, NP),
             blocks(NP), blocks(NP), blocks(11), blocks(4), blocks(4),
@@ -398,6 +418,8 @@
             pltpu.VMEM((2, 16, W), BF16),
             pltpu.SemaphoreType.DMA((8,)), pltpu.SemaphoreType.DMA((COPIES,)), pltpu.SemaphoreType.DMA((COPIES,)),
             pltpu.SemaphoreType.DMA((NP,)), pltpu.SemaphoreType.DMA((NP,)),
+            pltpu.SemaphoreType.DMA((NP,)), pltpu.SemaphoreType.DMA((NP,)),
+            pltpu.SemaphoreType.DMA((11,)), pltpu.SemaphoreType.DMA((11,)),
         ],
         compiler_params=pltpu.CompilerParams(
             collective_id=0, has_side_effects=True, vmem_limit_bytes=60 * 2**20
@@ -414,8 +436,8 @@
         in_specs=[hbm] * 5,
         out_specs=[hbm] * 3,
         scratch_shapes=[
-            pltpu.VMEM((TOKENS, D2), BF16), pltpu.VMEM((TOKENS, W), BF16), pltpu.VMEM((TOKENS, W), BF16),
-            pltpu.VMEM((2, TOKENS, W), BF16), pltpu.VMEM((TD, D2), BF16),
+            pltpu.VMEM((D2, TOKENS), BF16), pltpu.VMEM((TOKENS, W), BF16), pltpu.VMEM((TOKENS, W), BF16),
+            pltpu.VMEM((D2, TOKENS), BF16), pltpu.VMEM((TD, D2), BF16),
             pltpu.VMEM((D2, W), F32), pltpu.VMEM((D2, W), F32),
             pltpu.SemaphoreType.DMA((5,)), pltpu.SemaphoreType.DMA((5,)),
         ],

time: 82.2 us -> 80.8 us (0.983); the launches traced: 82 us -> 79.7 us
  Pallas kernels: 81.4 us -> 79 us
    pallas_call x1, Pallas kernels: 77.7 us -> 75.4 us  [shards(): pl.pallas_call(kernel, name='feed_forward_backward', out_shape=[jax.Shape...]
where the time goes in v3:
time: 80.8 us; the launch traced here: 79.7 us
  Pallas kernels  79 us (98%)
    pallas_call x1, Pallas kernels, shards(): pl.pallas_call(kernel, name='feed_forward_backward', out_shape=[jax.Shape...  75.4 us
    pallas_call x1, Pallas kernels, shards(): pl.pallas_call(products, name='weight_gradients', out_shape=[jax.ShapeDty...  3.62 us

profile of v3, /device:TPU:1, one launch (start us, length us, event | category | flops | bytes accessed | tf_op | source)
XLA Modules:
  0.0 79.7 jit_solution(2102966471466384613)
XLA Ops:
  0.6 75.4 %feed_forward_backward.1 = (bf16[928,384]{1,0:T(8,128)(2,1)}, bf16[384,464]{1,0:T(8,128)(2,1)}, bf16[384,464]{1,0:T(8,128)(2,1)}, bf16[928,384]{1,0:T(8,128)(2,1)}, bf16[12,928]{1,0:T(8,128)(2,1)}) custom-call(bf16[12,928]{1,0:T(8,128)(2,1)} %x_hbm.1, bf16[24,464]{1,0:T(8,128)(2,1)} %dy_hbm.1, bf16[928,464]{1,0:T(8,128)(2,1)} %wu_hbm.1, bf16[928,464]{1,0:T(8,128)(2,1)} %wd_hbm.1), custom_call_target="tpu_custom_call" | custom-call | tf_op jit(solution)/shard_map/feed_forward_backward/pallas_call | solution.py:399
  76.0 3.6 %weight_gradients.1 = (bf16[12,928]{1,0:T(8,128)(2,1)}, f32[928,464]{1,0:T(8,128)}, f32[928,464]{1,0:T(8,128)}) custom-call(bf16[928,384]{1,0:T(8,128)(2,1)} %get-tuple-element.8.xd_hbm, bf16[384,464]{1,0:T(8,128)(2,1)} %get-tuple-element.9.dyd_hbm, bf16[384,464]{1,0:T(8,128)(2,1)} %get-tuple-element.10.hgd_hbm, bf16[928,384]{1,0:T(8,128)(2,1)} %get-tuple-element.11.act_hbm, ...), custom_call_target="tpu_custom_call" | custom-call | tf_op jit(solution)/shard_map/weight_gradients/pallas_call | solution.py:428

commit v4 on v3

--- a/solution.py
+++ b/solution.py
@@ -184,7 +184,6 @@
     to_sib = {0: [send(dyb.at[k, c], dyb.at[k, c], sib)], 1: [], 2: [], 3: []}
     x_sib = {0: send(xg.at[k, z], xg.at[k, z], sib)}
     wd_copy = send(wd_hbm.at[pl.ds(theirs, W)], wd_sib, sib)
-    wu_copy = send(wu_hbm.at[pl.ds(theirs, W)], wu_sib, sib)
 
     a_copies = {}
 
@@ -236,6 +235,7 @@
     forward(1)
     load_wd.wait()
     wd_copy.wait_recv()
+    wu_copy = send(wu_hbm.at[pl.ds(theirs, W)], wu_sib, sib)
     act_part(0)
     forward(3)
     act_part(1)
@@ -363,7 +363,10 @@
     xd_hbm, dyd_hbm, hgd_hbm, act_hbm, ig_hbm, ig_out, up_hbm, down_hbm,
     xd, dyd, hgd, act, ig, up, down, load_sems, sems,
 ):
-    pairs = ((ig_hbm, ig), (xd_hbm, xd), (hgd_hbm, hgd), (act_hbm, act), (dyd_hbm, dyd))
+    pairs = (
+        (ig_hbm, ig), (hgd_hbm, hgd), (xd_hbm.at[0:512], xd.at[0:512]), (xd_hbm.at[512:D2], xd.at[512:D2]),
+        (dyd_hbm, dyd), (act_hbm.at[0:W], act.at[0:W]), (act_hbm.at[W:D2], act.at[W:D2]),
+    )
     loads = [pltpu.make_async_copy(a, b, load_sems.at[n]) for n, (a, b) in enumerate(pairs)]
     for load in loads:
         load.start()
@@ -376,15 +379,17 @@
     loads[0].wait()
     write(ig, ig_out)
     loads[1].wait()
-    loads[2].wait()
-    for low, high in ((0, 512), (512, D2)):
+    for n, (low, high) in enumerate(((0, 512), (512, D2))):
+        loads[2 + n].wait()
         up[low:high, :] = dot(xd[low:high, :], hgd[...])
         write(up.at[low:high], up_hbm.at[low:high])
-    loads[3].wait()
     loads[4].wait()
-    for n in range(2):
-        down[n * W : n * W + W, :] = dot(act[n * W : n * W + W, :], dyd[...])
-        write(down.at[n * W : n * W + W], down_hbm.at[n * W : n * W + W])
+    loads[5].wait()
+    for low, high in ((0, W), (W, 768), (768, D2)):
+        if low == W:
+            loads[6].wait()
+        down[low:high, :] = dot(act[low:high, :], dyd[...])
+        write(down.at[low:high], down_hbm.at[low:high])
     for copy in copies:
         copy.wait()
 
@@ -439,7 +444,7 @@
             pltpu.VMEM((D2, TOKENS), BF16), pltpu.VMEM((TOKENS, W), BF16), pltpu.VMEM((TOKENS, W), BF16),
             pltpu.VMEM((D2, TOKENS), BF16), pltpu.VMEM((TD, D2), BF16),
             pltpu.VMEM((D2, W), F32), pltpu.VMEM((D2, W), F32),
-            pltpu.SemaphoreType.DMA((5,)), pltpu.SemaphoreType.DMA((5,)),
+            pltpu.SemaphoreType.DMA((7,)), pltpu.SemaphoreType.DMA((6,)),
         ],
         compiler_params=pltpu.CompilerParams(vmem_limit_bytes=60 * 2**20),
     )(*gathered)

time: 80.8 us -> 80.5 us (level)
  no operation moved by 1% of the time
where the time goes in v4:
time: 80.5 us; the launch traced here: 79.8 us
  Pallas kernels  79.2 us (98%)
    pallas_call x1, Pallas kernels, shards(): pl.pallas_call(kernel, name='feed_forward_backward', out_shape=[jax.Shape...  75.5 us
    pallas_call x1, Pallas kernels, shards(): pl.pallas_call(products, name='weight_gradients', out_shape=[jax.ShapeDty...  3.73 us

profile of v4, /device:TPU:1, one launch (start us, length us, event | category | flops | bytes accessed | tf_op | source)
XLA Modules:
  0.0 79.8 jit_solution(1264625858314200893)
XLA Ops:
  0.6 75.5 %feed_forward_backward.1 = (bf16[928,384]{1,0:T(8,128)(2,1)}, bf16[384,464]{1,0:T(8,128)(2,1)}, bf16[384,464]{1,0:T(8,128)(2,1)}, bf16[928,384]{1,0:T(8,128)(2,1)}, bf16[12,928]{1,0:T(8,128)(2,1)}) custom-call(bf16[12,928]{1,0:T(8,128)(2,1)} %x_hbm.1, bf16[24,464]{1,0:T(8,128)(2,1)} %dy_hbm.1, bf16[928,464]{1,0:T(8,128)(2,1)} %wu_hbm.1, bf16[928,464]{1,0:T(8,128)(2,1)} %wd_hbm.1), custom_call_target="tpu_custom_call" | custom-call | tf_op jit(solution)/shard_map/feed_forward_backward/pallas_call | solution.py:404
  76.1 3.7 %weight_gradients.1 = (bf16[12,928]{1,0:T(8,128)(2,1)}, f32[928,464]{1,0:T(8,128)}, f32[928,464]{1,0:T(8,128)}) custom-call(bf16[928,384]{1,0:T(8,128)(2,1)} %get-tuple-element.8.xd_hbm, bf16[384,464]{1,0:T(8,128)(2,1)} %get-tuple-element.9.dyd_hbm, bf16[384,464]{1,0:T(8,128)(2,1)} %get-tuple-element.10.hgd_hbm, bf16[928,384]{1,0:T(8,128)(2,1)} %get-tuple-element.11.act_hbm, ...), custom_call_target="tpu_custom_call" | custom-call | tf_op jit(solution)/shard_map/weight_gradients/pallas_call | solution.py:433
